TPU v7x, 32 devices: a whole 2x2x4 slice. The times are simulated.
32 devices in a mesh: set: 1, kb: 32 (over z, y, x, core).
Axes of the slice: x: 2, y: 2, z: 4, core: 2. Of those that a mesh axis runs over, the one named last changes fastest.
Arguments:
- green_momentum_grid: float32 [2, 4, 4096, 512], P('set', None, 'kb'), may hold values from -6 to 6
- pair_table: int32 [8, 2], replicated, may hold values from 0 to 3, as said below
- mirror_map: int32 [3, 16], P('set'), may hold values from 0 to 15, as said below
Outputs:
- chi_out: float32 [2, 8, 4096, 512], P('set', None, 'kb')
Inputs may be any that keep to these rules, and one draw needn't show every extreme that they name: `pair_table`: each of the two columns names every entry number 0 to 3 at least once. Each row d is a reflection: mirror_map[d,x] = (c_d - x) mod 16 for a centre c_d of that row.
All inputs are finite; a program needn't handle non-finite values.
Results may differ from a plain program's by a relative error of at most 0.0003.
Values sent between devices are 32-bit elements; how exact they have to be, the bound alone decides.
A program may use at most 128 MiB of HBM per device.

v0:
```python
import functools

import numpy as np
import ml_dtypes
import jax
import jax.numpy as jnp
from jax import lax
from jax.experimental import pallas as pl
from jax.experimental.pallas import tpu as pltpu
from jax.sharding import PartitionSpec as P

CHUNKS = 2
SMEM = pl.BlockSpec(memory_space=pltpu.SMEM)


def split_np(table):
    table = table.astype(np.float32)
    high = table.astype(ml_dtypes.bfloat16)
    low = (table - high.astype(np.float32)).astype(ml_dtypes.bfloat16)
    return high, low


def split(x):
    high = x.astype(jnp.bfloat16)
    return high, (x - high.astype(jnp.float32)).astype(jnp.bfloat16)


def mm(a, b, dims):
    return lax.dot_general(a, b, (dims, ((), ())), preferred_element_type=jnp.float32)


def mm3(a, b, dims=((1,), (0,))):
    return mm(a[0], b[0], dims) + mm(a[1], b[0], dims) + mm(a[0], b[1], dims)


def owned_times(devices, freqs, chunk):
    per = freqs // (2 * CHUNKS * devices)
    first = chunk * (freqs // (2 * CHUNKS)) + np.arange(devices)[:, None] * per + np.arange(per)[None, :]
    return np.stack([first, freqs - 1 - first], axis=1).reshape(-1)


def time_tables(times, freqs):
    angle = ((2 * np.arange(freqs)[None, :] - freqs + 1) * (2 * times[:, None] + 1)) % (4 * freqs)
    angle = angle * (2 * np.pi / (4 * freqs))
    scale = freqs**-0.5
    return split_np(scale * np.cos(angle)) + split_np(scale * np.sin(angle))


def frequency_tables(times, freqs):
    angle = ((np.arange(freqs)[None, :] - freqs // 2) * (2 * times[:, None] + 1)) % (2 * freqs)
    angle = angle * (2 * np.pi / (2 * freqs))
    cos, sin = np.cos(angle) * freqs**-0.5, np.sin(angle) * freqs**-0.5
    return split_np(np.block([[cos, sin], [-sin, cos]]))


def plane_table(side, sign):
    index = np.arange(side * side)
    upper, lower = index // side, index % side
    angle = (upper[:, None] * upper[None, :] + lower[:, None] * lower[None, :]) % side * (2 * np.pi / side)
    scale = (side**3) ** -0.5
    cos, sin = scale * np.cos(angle), sign * scale * np.sin(angle)
    return split_np(np.block([[cos, sin], [-sin, cos]]))


def cadd(a, b):
    return a[0] + b[0], a[1] + b[1]


def csub(a, b):
    return a[0] - b[0], a[1] - b[1]


def dft4(a, sign):
    s02, d02 = cadd(a[0], a[2]), csub(a[0], a[2])
    s13, d13 = cadd(a[1], a[3]), csub(a[1], a[3])
    turned = (-d13[1], d13[0]) if sign > 0 else (d13[1], -d13[0])
    return [cadd(s02, s13), cadd(d02, turned), csub(s02, s13), csub(d02, turned)]


def twiddle(a, power, sign):
    if power == 0:
        return a
    if power == 4:
        return (-a[1], a[0]) if sign > 0 else (a[1], -a[0])
    if power in (2, 6):
        r = np.float32(np.sqrt(0.5))
        plus, minus = (a[0] + a[1]) * r, (a[0] - a[1]) * r
        if power == 2:
            return (minus, plus) if sign > 0 else (plus, -minus)
        return (-plus, minus) if sign > 0 else (-minus, -plus)
    c = np.float32(np.cos(2 * np.pi * power / 16))
    s = np.float32(sign * np.sin(2 * np.pi * power / 16))
    return a[0] * c - a[1] * s, a[0] * s + a[1] * c


def dft16(x, sign):
    columns = [dft4([x[4 * n1 + n2] for n1 in range(4)], sign) for n2 in range(4)]
    out = [None] * 16
    for k1 in range(4):
        row = dft4([twiddle(columns[n2][k1], n2 * k1, sign) for n2 in range(4)], sign)
        for k2 in range(4):
            out[k1 + 4 * k2] = row[k2]
    return out


def to_time(g_ref, table, o_ref, p):
    devices, _, entries, slots, points = o_ref.shape[1:]
    freqs = g_ref.shape[-1]
    cos, sin = (table[p, 0], table[p, 1]), (table[p, 2], table[p, 3])
    dims = ((1,), (1,))
    re = split(g_ref[0].reshape(entries * points, freqs))
    im = split(g_ref[1].reshape(entries * points, freqs))
    tau = (mm3(cos, re, dims) + mm3(sin, im, dims), mm3(cos, im, dims) - mm3(sin, re, dims))
    for part in range(2):
        for e in range(entries):
            o_ref[p, :, part, e] = tau[part][:, e * points:(e + 1) * points].reshape(devices, slots, points)


def bubble(pair_ref, mirror_ref, x_ref, ahead, mirrored, inverse, o_ref, y, g, gm, chi, p):
    devices, _, entries, slots, points = x_ref.shape[1:]
    side = y.shape[0]
    plane = side * side
    halves = devices // side
    comps = o_ref.shape[3]

    def forth(e, carry):
        for h in range(halves):
            cells = [(x_ref[p, k * halves + h, 0, e], x_ref[p, k * halves + h, 1, e]) for k in range(side)]
            for k, (re, im) in enumerate(dft16(cells, 1)):
                y[k, e, :, h * points:(h + 1) * points] = re
                y[k, e, :, plane + h * points:plane + (h + 1) * points] = im
        return carry

    lax.fori_loop(0, entries, forth, 0)
    rows = split(y[...].reshape(side * entries * slots, 2 * plane))
    g[...] = mm3(rows, (ahead[0], ahead[1])).reshape(g.shape)
    other = mm3(rows, (mirrored[0], mirrored[1])).reshape(side * entries, slots, 2 * plane)
    other = jnp.concatenate([other[:, slots // 2:], other[:, :slots // 2]], axis=1)
    gm[...] = other.reshape(gm.shape)

    def one(c, carry):
        left, right = pair_ref[0, c], pair_ref[1, c]
        for r in range(side):
            a = g[r, left]
            b = gm[mirror_ref[0, r], right]
            ar, ai, br, bi = a[:, :plane], a[:, plane:], b[:, :plane], b[:, plane:]
            chi[c, r, :, :plane] = ar * br - ai * bi
            chi[c, r, :, plane:] = ar * bi + ai * br
        return carry

    lax.fori_loop(0, comps, one, 0)
    rows = split(chi[...].reshape(comps * side * slots, 2 * plane))
    chi[...] = mm3(rows, (inverse[0], inverse[1])).reshape(chi.shape)

    def back(c, carry):
        for h in range(halves):
            lanes = slice(h * points, (h + 1) * points)
            high = slice(plane + h * points, plane + (h + 1) * points)
            cells = [(chi[c, r, :, lanes], chi[c, r, :, high]) for r in range(side)]
            for q, (re, im) in enumerate(dft16(cells, -1)):
                o_ref[p, q * halves + h, 0, c] = re
                o_ref[p, q * halves + h, 1, c] = im
        return carry

    lax.fori_loop(0, comps, back, 0)


def main_kernel(pair_ref, mirror_ref, green_hbm, time_hbm, plane_hbm, back_hbm, half_hbm, last,
                green, table, planes, back, mirrored, tau, x, y, g, gm, chi, sent, got, acc,
                load, own, send, recv):
    devices = tau.shape[1]
    side = y.shape[0]
    plane = side * side
    me = lax.axis_index("kb")
    loads = [pltpu.make_async_copy(src, dst, load.at[i])
             for i, (src, dst) in enumerate([(time_hbm, table), (plane_hbm, planes), (back_hbm, back),
                                       (green_hbm, green)])]
    for i in (3, 0, 1, 2):
        loads[i].start()
    barrier = pltpu.get_barrier_semaphore()

    def greet(s, carry):
        pl.semaphore_signal(barrier, inc=1, device_id={"kb": lax.rem(me + s, devices)},
                            device_id_type=pl.DeviceIdType.MESH)
        return carry

    lax.fori_loop(1, devices, greet, 0)

    def partner(shift):
        total, bit = 0, 1
        while bit < devices:
            total += bit * lax.rem(me // bit + shift // bit, 2)
            bit *= 2
        return total

    def exchange(src, dst, n):
        pltpu.make_async_copy(src.at[me], dst.at[me], own.at[n]).start()

        def one(i, carry):
            other = partner(i // 4 + devices // 4 * lax.rem(i + 2, 4))
            pltpu.make_async_remote_copy(
                src_ref=src.at[other], dst_ref=dst.at[me], send_sem=send.at[n], recv_sem=recv.at[n],
                device_id={"kb": other}, device_id_type=pl.DeviceIdType.MESH,
            ).start()
            return carry

        lax.fori_loop(0, 2, one, 0)
        lax.fori_loop(3, devices, one, 0)

    def finish(ref, sem):
        part = ref.at[pl.ds(0, devices - 1)]
        pltpu.make_async_copy(part, part, sem).wait()

    loads[3].wait()
    loads[0].wait()
    for p in range(CHUNKS):
        to_time(green, table, tau, p)
        if p == 0:
            pl.semaphore_wait(barrier, devices - 1)
        exchange(tau.at[p], x.at[p], p)
    loads[1].wait()
    lane = lax.broadcasted_iota(jnp.int32, (plane, plane), 1)
    ry, rz = lane // side, lane % side
    target = (mirror_ref[1, 0] + side - ry) % side * side + (mirror_ref[2, 0] + side - rz) % side
    pick = (lax.broadcasted_iota(jnp.int32, (plane, plane), 0) == target).astype(jnp.float32).astype(jnp.bfloat16)
    for i in range(2):
        for part in range(2):
            lanes = slice(part * plane, (part + 1) * plane)
            mirrored[i, :, lanes] = mm(planes[i, :, lanes], pick, ((1,), (0,))).astype(jnp.bfloat16)
    landing = [got, last]
    for p in range(CHUNKS):
        pltpu.make_async_copy(tau.at[p, me], x.at[p, me], own.at[p]).wait()
        finish(x.at[p], recv.at[p])
        bubble(pair_ref, mirror_ref, x, planes.at[0:2], mirrored, planes.at[2:4], sent, y, g, gm, chi, p)
        exchange(sent.at[p], landing[p], CHUNKS + p)
    pltpu.make_async_copy(sent.at[0, me], got.at[me], own.at[CHUNKS]).wait()
    finish(got, recv.at[CHUNKS])
    loads[2].wait()
    comps = got.shape[2]
    block = comps // 2
    for i in range(2):
        chosen = slice(i * block, (i + 1) * block)
        value = to_frequency(got.at[:, :, chosen], back)
        for part in range(2):
            acc[part, chosen] = value[part]
    store = pltpu.make_async_copy(acc, half_hbm, load.at[4])
    store.start()
    for p in range(CHUNKS):
        finish(tau.at[p], send.at[p])
        finish(sent.at[p], send.at[CHUNKS + p])
    store.wait()
    pltpu.make_async_copy(sent.at[1, me], last.at[me], own.at[CHUNKS + 1]).wait()
    finish(last, recv.at[CHUNKS + 1])


def to_frequency(x_ref, b_ref):
    devices, _, block, slots, points = x_ref.shape
    freqs = b_ref.shape[-1] // 2
    rows = []
    for c in range(block):
        parts = [x_ref[:, part, c].reshape(devices * slots, points).T for part in range(2)]
        rows.append(jnp.concatenate(parts, axis=1))
    value = mm3(split(jnp.concatenate(rows, axis=0)), (b_ref[0], b_ref[1]))
    return [value[:, part * freqs:(part + 1) * freqs].reshape(block, points, freqs) for part in range(2)]


def finish_kernel(x_ref, b_ref, half_ref, o_ref):
    value = to_frequency(x_ref, b_ref)
    for part in range(2):
        o_ref[part] = half_ref[part] + value[part]


def local(devices, green, pair_table, mirror_map):
    entries, points, freqs = green.shape[1:]
    side = mirror_map.shape[1]
    plane = side * side
    comps = pair_table.shape[0]
    slots = freqs // (devices * CHUNKS)
    f32, bf16 = jnp.float32, jnp.bfloat16
    times = [owned_times(devices, freqs, p) for p in range(CHUNKS)]
    time_table = np.stack([np.stack(time_tables(t, freqs)) for t in times])
    plane_tables = np.stack(plane_table(side, 1.0) + plane_table(side, -1.0))
    frequency_table = [np.stack(frequency_tables(t, freqs)) for t in times]
    hbm = pl.BlockSpec(memory_space=pl.ANY)
    cells = (side, entries, slots, 2 * plane)
    exchanged = (devices, 2, comps, slots, points)
    result = (2, comps, points, freqs)
    half, last = pl.pallas_call(
        main_kernel,
        out_shape=[jax.ShapeDtypeStruct(result, f32), jax.ShapeDtypeStruct(exchanged, f32)],
        in_specs=[SMEM, SMEM, hbm, hbm, hbm, hbm],
        out_specs=[hbm, hbm],
        scratch_shapes=[
            pltpu.VMEM(green.shape, f32),
            pltpu.VMEM(time_table.shape, bf16),
            pltpu.VMEM(plane_tables.shape, bf16),
            pltpu.VMEM(frequency_table[0].shape, bf16),
            pltpu.VMEM((2, 2 * plane, 2 * plane), bf16),
            pltpu.VMEM((CHUNKS, devices, 2, entries, slots, points), f32),
            pltpu.VMEM((CHUNKS, devices, 2, entries, slots, points), f32),
            pltpu.VMEM(cells, f32),
            pltpu.VMEM(cells, f32),
            pltpu.VMEM(cells, f32),
            pltpu.VMEM((comps,) + (side, slots, 2 * plane), f32),
            pltpu.VMEM((CHUNKS,) + exchanged, f32),
            pltpu.VMEM(exchanged, f32),
            pltpu.VMEM(result, f32),
            pltpu.SemaphoreType.DMA((5,)),
            pltpu.SemaphoreType.DMA((2 * CHUNKS,)),
            pltpu.SemaphoreType.DMA((2 * CHUNKS,)),
            pltpu.SemaphoreType.DMA((2 * CHUNKS,)),
        ],
        compiler_params=pltpu.CompilerParams(
            vmem_limit_bytes=60 * 1024 * 1024, collective_id=0, has_side_effects=True
        ),
        cost_estimate=pl.CostEstimate(flops=18 * 10**9, bytes_accessed=16 * 2**20, transcendentals=0),
    )(pair_table.T, mirror_map, green, time_table, plane_tables, frequency_table[0])
    block = comps // 4
    whole = pl.BlockSpec((2, block, points, freqs), lambda i: (0, i, 0, 0))
    return pl.pallas_call(
        finish_kernel,
        grid=(comps // block,),
        out_shape=jax.ShapeDtypeStruct(result, f32),
        in_specs=[
            pl.BlockSpec((devices, 2, block, slots, points), lambda i: (0, 0, i, 0, 0)),
            pl.BlockSpec(frequency_table[1].shape, lambda i: (0, 0, 0)),
            whole,
        ],
        out_specs=whole,
        compiler_params=pltpu.CompilerParams(vmem_limit_bytes=58 * 1024 * 1024),
        cost_estimate=pl.CostEstimate(flops=6 * 10**9, bytes_accessed=16 * 2**20, transcendentals=0),
    )(last, frequency_table[1], half)


def solution(mesh):
    placed = (P("set", None, "kb", None), P(), P("set", None))
    return jax.shard_map(
        functools.partial(local, mesh.shape["kb"]),
        mesh=mesh,
        in_specs=placed,
        out_specs=P("set", None, "kb", None),
        check_vma=False,
    )
```

profile of v0, /device:TPU:0, one launch (start us, length us, event | category | flops | bytes accessed | tf_op | source)
XLA Modules:
  0.0 152.7 jit_solution(9875759316672152520)
XLA Ops:
  0.0 144.6 %shard_map.73 = (f32[2,8,128,512]{3,2,1,0:T(8,128)}, f32[32,2,8,8,128]{4,3,2,1,0:T(8,128)}) custom-call(s32[2,8]{1,0:T(2,128)} %bitcast.1, s32[3,16]{1,0:T(4,128)} %mirror_ref.1, f32[2,4,128,512]{3,2,1,0:T(8,128)} %green_hbm.1, bf16[2,4,256,512]{3,2,1,0:T(8,128)(2,1)} %constant.8.clone.time_hbm, bf16[4,512,512]{2,1,0:T(8,128)(2,1)} %constant.9.clone.plane_hbm, ...), custom_call_target="tpu_custom_call" | custom-call | flops 17999998976 | bytes 16777216 | tf_op jit(solution)/shard_map/pallas_call | solution.py:288
  144.6 8.1 %shard_map.74 = f32[2,8,128,512]{3,2,1,0:T(8,128)} custom-call(f32[32,2,8,8,128]{4,3,2,1,0:T(8,128)} %get-tuple-element.7.x_ref, bf16[2,512,1024]{2,1,0:T(8,128)(2,1)} %constant.11.clone.b_ref, f32[2,8,128,512]{3,2,1,0:T(8,128)} %get-tuple-element.8.half_ref), custom_call_target="tpu_custom_call" | custom-call | flops 6000000000 | bytes 16777216 | tf_op jit(solution)/shard_map/pallas_call | solution.py:320
where the time goes:
time: 154 us; the launch traced here: 153 us
  Pallas kernels  153 us (99%)
    pallas_call x1, Pallas kernels, local(): pl.pallas_call(main_kernel, out_shape=[jax.ShapeDtypeStruct(result, f32),...  145 us
    pallas_call x1, Pallas kernels, local(): pl.pallas_call(finish_kernel, grid=(comps // block,), out_shape=jax.Shape...  8.11 us

commit v1 on v0

--- a/solution.py
+++ b/solution.py
@@ -332,10 +332,398 @@
     )(last, frequency_table[1], half)
 
 
+LEVELS = 4
+PIECES = 8
+LEAD = 3
+GROUP = 2
+
+
+def piece_times(members, freqs, piece):
+    per = freqs // (2 * PIECES * members)
+    first = piece * (freqs // (2 * PIECES)) + np.arange(members)[:, None] * per + np.arange(per)[None, :]
+    return np.stack([first, freqs - 1 - first], axis=1).reshape(-1)
+
+
+def stacked_time_table(times, freqs):
+    cos_high, cos_low, sin_high, sin_low = time_tables(times, freqs)
+    return np.concatenate([cos_high, sin_high, cos_low, sin_low])
+
+
+def group_table(members, freqs, group):
+    rows = []
+    for piece in range(group * GROUP, (group + 1) * GROUP):
+        times = piece_times(members, freqs, piece)
+        angle = ((np.arange(freqs)[None, :] - freqs // 2) * (2 * times[:, None] + 1)) % (2 * freqs)
+        angle = angle * (2 * np.pi / (2 * freqs))
+        cos, sin = np.cos(angle) * freqs**-0.5, np.sin(angle) * freqs**-0.5
+        rows.append(np.block([[cos, sin], [-sin, cos]]))
+    return np.stack(split_np(np.concatenate(rows)))
+
+
+def mm3s(rows, high, low):
+    m = rows.shape[0]
+    a, b = split(rows)
+    both = mm(jnp.concatenate([a, b], axis=0), high, ((1,), (0,)))
+    return both[:m] + both[m:] + mm(a, low, ((1,), (0,)))
+
+
+def dft16_half(columns, sigma):
+    out = [None] * 8
+    for k1 in range(4):
+        a = [twiddle(columns[n2][k1], n2 * k1, -1) for n2 in range(4)]
+        s02, d02 = cadd(a[0], a[2]), csub(a[0], a[2])
+        s13, d13 = cadd(a[1], a[3]), csub(a[1], a[3])
+        out[k1] = (s02[0] + sigma * s13[0], s02[1] + sigma * s13[1])
+        out[4 + k1] = (d02[0] + sigma * d13[1], d02[1] - sigma * d13[0])
+    return out
+
+
+def level_kernel(pair_ref, mirror_ref, green_hbm, time_hbm, plane_hbm, back_hbm, half_hbm, last,
+                 green, table, planes, back, mirrored, tau, x, zbuf, t, ts, chi, sent, got, acc,
+                 load, own, send, recv1, recvz, recvc, recv2):
+    members = tau.shape[1]
+    entries, slots, points = tau.shape[3:]
+    side = t.shape[0]
+    lines = side // LEVELS
+    plane = side * side
+    comps = sent.shape[3]
+    freqs = green.shape[-1]
+    kept = got.shape[0]
+    me = lax.axis_index("kb")
+    z, d = me // members, lax.rem(me, members)
+    middle = jnp.logical_or(z == 1, z == 2)
+    edge = jnp.logical_not(middle)
+    mine = lax.rem(z, 2)
+    half = slots // 2
+
+    loads = [pltpu.make_async_copy(src, dst, load.at[i])
+             for i, (src, dst) in enumerate([(time_hbm, table), (plane_hbm, planes), (back_hbm, back),
+                                             (green_hbm, green)])]
+    for i in (3, 0, 1, 2):
+        loads[i].start()
+    barrier = pltpu.get_barrier_semaphore()
+
+    def greet(other):
+        pl.semaphore_signal(barrier, inc=1, device_id={"kb": other}, device_id_type=pl.DeviceIdType.MESH)
+
+    def greet_member(s, carry):
+        greet(z * members + lax.rem(d + s, members))
+        return carry
+
+    lax.fori_loop(1, members, greet_member, 0)
+    for s in range(1, LEVELS):
+        greet(lax.rem(z + s, LEVELS) * members + d)
+
+    def partner(shift):
+        total, bit = 0, 1
+        while bit < members:
+            total += bit * lax.rem(d // bit + shift // bit, 2)
+            bit *= 2
+        return total
+
+    def remote(src, dst, send_sem, recv_sem, other):
+        pltpu.make_async_remote_copy(
+            src_ref=src, dst_ref=dst, send_sem=send_sem, recv_sem=recv_sem,
+            device_id={"kb": other}, device_id_type=pl.DeviceIdType.MESH,
+        ).start()
+
+    def exchange(src, dst, own_sem, send_sem, recv_sem):
+        pltpu.make_async_copy(src.at[d], dst.at[d], own_sem).start()
+
+        def one(i, carry):
+            other = partner(members - i)
+            remote(src.at[other], dst.at[d], send_sem, recv_sem, z * members + other)
+            return carry
+
+        lax.fori_loop(1, members, one, 0)
+
+    def drain(ref, sem):
+        pltpu.make_async_copy(ref, ref, sem).wait()
+
+    def finish(src, dst, own_sem, recv_sem):
+        pltpu.make_async_copy(src.at[d], dst.at[d], own_sem).wait()
+        drain(dst.at[pl.ds(0, members - 1)], recv_sem)
+
+    loads[3].wait()
+    loads[0].wait()
+    stacks = table.shape[0]
+    per = PIECES // stacks
+    times = freqs // stacks
+    dims = ((1,), (1,))
+    re = split(green[0].reshape(entries * points, freqs))
+    im = split(green[1].reshape(entries * points, freqs))
+    for s in range(stacks):
+        outs = []
+        for value in (re, im):
+            a = mm(table[s], value[0], dims)
+            outs.append(a[:2 * times] + a[2 * times:] + mm(table[s, :2 * times], value[1], dims))
+        both = (outs[0][:times] + outs[1][times:], outs[1][:times] - outs[0][times:])
+        for part in range(2):
+            for e in range(entries):
+                tau[s * per:(s + 1) * per, :, part, e] = both[part][:, e * points:(e + 1) * points].reshape(
+                    per, members, slots, points)
+        if s == 0:
+            pl.semaphore_wait(barrier, members - 1 + LEVELS - 1)
+
+        def out(p, carry):
+            exchange(tau.at[p], x.at[p], own.at[p], send.at[0], recv1.at[p])
+            return carry
+
+        lax.fori_loop(s * per, (s + 1) * per, out, 0)
+    loads[1].wait()
+    lane = lax.broadcasted_iota(jnp.int32, (plane, plane), 1)
+    ry, rz = lane // side, lane % side
+    target = (mirror_ref[1, 0] + side - ry) % side * side + (mirror_ref[2, 0] + side - rz) % side
+    pick = (lax.broadcasted_iota(jnp.int32, (plane, plane), 0) == target).astype(jnp.float32).astype(jnp.bfloat16)
+    for i in range(2):
+        for part in range(2):
+            lanes = slice(part * plane, (part + 1) * plane)
+            mirrored[i, :, lanes] = mm(planes[i, :, lanes], pick, ((1,), (0,))).astype(jnp.bfloat16)
+            mirrored[2 + i, lanes, :] = mm(pick, planes[2 + i, lanes, :], ((1,), (0,))).astype(jnp.bfloat16)
+
+    def both_ways(rows, base):
+        straight = mm3s(rows, planes[base], planes[base + 1])
+        turned = mm3s(rows, mirrored[base], mirrored[base + 1])
+        slot = lax.broadcasted_iota(jnp.int32, straight.shape, 0) % slots
+        return jnp.where(slot < half, straight, turned)
+
+    def forward(p):
+        finish(tau.at[p], x.at[p], own.at[p], recv1.at[p])
+        v = x[p].reshape(lines, 2, 2, entries, slots, points)
+        rows = jnp.concatenate([v[:, h, part].reshape(lines * entries * slots, points)
+                                for part in range(2) for h in range(2)], axis=1)
+        out = both_ways(rows, 0)
+        for h in range(2):
+            for part in range(2):
+                lanes = slice(part * plane + h * points, part * plane + (h + 1) * points)
+                zbuf[p, h, z, part] = out[:, lanes].reshape(lines, entries, slots, points)
+            for level in (1, 2):
+                @pl.when(z != level)
+                def _():
+                    remote(zbuf.at[p, h, z], zbuf.at[p, h, z], send.at[1], recvz.at[p, h], level * members + d)
+
+    def middle_work(p, h):
+        drain(zbuf.at[p, h, pl.ds(0, LEVELS - 1)], recvz.at[p, h])
+        sigma = jnp.where(z == 1, 1.0, -1.0).astype(jnp.float32)
+
+        def forth(e, carry):
+            cells = [(zbuf[p, h, k // lines, 0, k % lines, e], zbuf[p, h, k // lines, 1, k % lines, e])
+                     for k in range(side)]
+            for r, pair in enumerate(dft16(cells, 1)):
+                for part in range(2):
+                    v = pair[part]
+                    t[r, e, part] = v
+                    ts[r, e, part] = jnp.concatenate([v[half:], v[:half]], axis=0)
+            return carry
+
+        lax.fori_loop(0, entries, forth, 0)
+
+        def one(c, carry):
+            left, right = pair_ref[0, c], pair_ref[1, c]
+            columns = []
+            for n2 in range(4):
+                cells = []
+                for n1 in range(4):
+                    r = 4 * n1 + n2
+                    a, b = t[r, left], ts[mirror_ref[0, r], right]
+                    cells.append((a[0] * b[0] - a[1] * b[1], a[0] * b[1] + a[1] * b[0]))
+                columns.append(dft4(cells, -1))
+            for i, pair in enumerate(dft16_half(columns, sigma)):
+                for part in range(2):
+                    chi[i // lines, p, h, c, part, i % lines] = pair[part]
+            remote(chi.at[1 - mine, p, h, c], chi.at[1 - mine, p, h, c], send.at[2], recvc.at[p],
+                   jnp.where(z == 1, 0, 3) * members + d)
+            return carry
+
+        lax.fori_loop(0, comps, one, 0)
+
+    def backward(p):
+        v = chi[mine, p]
+        rows = jnp.concatenate([v[h, :, part].reshape(comps * lines * slots, points)
+                                for part in range(2) for h in range(2)], axis=1)
+        out = both_ways(rows, 2).reshape(comps, lines, slots, 2 * plane)
+        for q in range(lines):
+            for h in range(2):
+                for part in range(2):
+                    lanes = slice(part * plane + h * points, part * plane + (h + 1) * points)
+                    sent[p, 2 * q + h, part] = out[:, q, :, lanes]
+
+    def frequency(m):
+        block = comps // 2
+        for i in range(2):
+            chosen = slice(i * block, (i + 1) * block)
+            value = mm3s(frequency_rows([got.at[m * GROUP + g] for g in range(GROUP)], i * block, block),
+                         back[m, 0], back[m, 1])
+            for part in range(2):
+                acc[part, chosen] += value[:, part * freqs:(part + 1) * freqs].reshape(block, points, freqs)
+
+    acc[...] = jnp.zeros(acc.shape, jnp.float32)
+    loads[2].wait()
+
+    def lead(p, carry):
+        forward(p)
+        return carry
+
+    lax.fori_loop(0, LEAD, lead, 0)
+
+    def step(p, carry):
+        @pl.when(p + LEAD < PIECES)
+        def _():
+            forward(p + LEAD)
+
+        @pl.when(jnp.logical_and(lax.rem(p, GROUP) == GROUP - 1, p >= 2 * GROUP - 1))
+        def _():
+            m = p // GROUP - 1
+
+            def arrived(q, carry):
+                finish(sent.at[q], got.at[q], own.at[PIECES + q], recv2.at[q])
+                return carry
+
+            lax.fori_loop(m * GROUP, (m + 1) * GROUP, arrived, 0)
+            frequency(m)
+
+        @pl.when(middle)
+        def _():
+            for h in range(2):
+                middle_work(p, h)
+
+        @pl.when(edge)
+        def _():
+            drain(chi.at[mine, p], recvc.at[p])
+
+        backward(p)
+
+        @pl.when(p < kept)
+        def _():
+            exchange(sent.at[p], got.at[p], own.at[PIECES + p], send.at[3], recv2.at[p])
+
+        @pl.when(p >= kept)
+        def _():
+            exchange(sent.at[p], last.at[p - kept], own.at[PIECES + p], send.at[3], recv2.at[p])
+
+        return carry
+
+    lax.fori_loop(0, PIECES, step, 0)
+    store = pltpu.make_async_copy(acc, half_hbm, load.at[4])
+    store.start()
+    drain(tau.at[:, pl.ds(0, members - 1)], send.at[0])
+    drain(zbuf.at[pl.ds(0, PIECES // LEVELS)], send.at[1])
+
+    @pl.when(edge)
+    def _():
+        drain(zbuf.at[pl.ds(0, PIECES // LEVELS)], send.at[1])
+
+    @pl.when(middle)
+    def _():
+        drain(chi.at[0], send.at[2])
+
+    for p in range(kept, PIECES):
+        finish(sent.at[p], last.at[p - kept], own.at[PIECES + p], recv2.at[p])
+    drain(sent.at[:, pl.ds(0, members - 1)], send.at[3])
+    store.wait()
+
+
+def frequency_rows(pieces, first, block):
+    rows = []
+    for c in range(first, first + block):
+        parts = []
+        for ref in pieces:
+            for part in range(2):
+                v = ref[:, part, c]
+                parts.append(v.reshape(v.shape[0] * v.shape[1], v.shape[2]))
+        rows.append(jnp.concatenate(parts, axis=0).T)
+    return jnp.concatenate(rows, axis=0)
+
+
+def level_finish(x_ref, b_ref, half_ref, o_ref):
+    block, points, freqs = o_ref.shape[1:]
+    value = mm3s(frequency_rows([x_ref.at[g] for g in range(GROUP)], 0, block), b_ref[0], b_ref[1])
+    for part in range(2):
+        o_ref[part] = half_ref[part] + value[:, part * freqs:(part + 1) * freqs].reshape(block, points, freqs)
+
+
+def level_local(devices, green, pair_table, mirror_map):
+    entries, points, freqs = green.shape[1:]
+    side = mirror_map.shape[1]
+    plane = side * side
+    comps = pair_table.shape[0]
+    members = devices // LEVELS
+    slots = freqs // (members * PIECES)
+    lines = side // LEVELS
+    f32, bf16 = jnp.float32, jnp.bfloat16
+    times = [piece_times(members, freqs, p) for p in range(PIECES)]
+    stacks = 2
+    per = PIECES // stacks
+    time_table = np.stack([stacked_time_table(np.concatenate(times[s * per:(s + 1) * per]), freqs)
+                           for s in range(stacks)])
+    plane_tables = np.stack(plane_table(side, 1.0) + plane_table(side, -1.0))
+    groups = PIECES // GROUP
+    back = [group_table(members, freqs, g) for g in range(groups)]
+    early = np.stack(back[:-1])
+    kept = PIECES - GROUP
+    hbm = pl.BlockSpec(memory_space=pl.ANY)
+    exchanged = (members, 2, comps, slots, points)
+    result = (2, comps, points, freqs)
+    cells = (side, entries, 2, slots, points)
+    half, last = pl.pallas_call(
+        level_kernel,
+        out_shape=[jax.ShapeDtypeStruct(result, f32), jax.ShapeDtypeStruct((GROUP,) + exchanged, f32)],
+        in_specs=[SMEM, SMEM, hbm, hbm, hbm, hbm],
+        out_specs=[hbm, hbm],
+        scratch_shapes=[
+            pltpu.VMEM(green.shape, f32),
+            pltpu.VMEM(time_table.shape, bf16),
+            pltpu.VMEM(plane_tables.shape, bf16),
+            pltpu.VMEM(early.shape, bf16),
+            pltpu.VMEM(plane_tables.shape, bf16),
+            pltpu.VMEM((PIECES, members, 2, entries, slots, points), f32),
+            pltpu.VMEM((PIECES, members, 2, entries, slots, points), f32),
+            pltpu.VMEM((PIECES, 2, LEVELS, 2, lines, entries, slots, points), f32),
+            pltpu.VMEM(cells, f32),
+            pltpu.VMEM(cells, f32),
+            pltpu.VMEM((2, PIECES, 2, comps, 2, lines, slots, points), f32),
+            pltpu.VMEM((PIECES,) + exchanged, f32),
+            pltpu.VMEM((kept,) + exchanged, f32),
+            pltpu.VMEM(result, f32),
+            pltpu.SemaphoreType.DMA((5,)),
+            pltpu.SemaphoreType.DMA((2 * PIECES,)),
+            pltpu.SemaphoreType.DMA((4,)),
+            pltpu.SemaphoreType.DMA((PIECES,)),
+            pltpu.SemaphoreType.DMA((PIECES, 2)),
+            pltpu.SemaphoreType.DMA((PIECES,)),
+            pltpu.SemaphoreType.DMA((PIECES,)),
+        ],
+        compiler_params=pltpu.CompilerParams(
+            vmem_limit_bytes=60 * 1024 * 1024, collective_id=0, has_side_effects=True
+        ),
+        cost_estimate=pl.CostEstimate(flops=18 * 10**9, bytes_accessed=16 * 2**20, transcendentals=0),
+    )(pair_table.T, mirror_map, green, time_table, plane_tables, early)
+    block = comps // 4
+    whole = pl.BlockSpec((2, block, points, freqs), lambda i: (0, i, 0, 0))
+    return pl.pallas_call(
+        level_finish,
+        grid=(comps // block,),
+        out_shape=jax.ShapeDtypeStruct(result, f32),
+        in_specs=[
+            pl.BlockSpec((GROUP, members, 2, block, slots, points), lambda i: (0, 0, 0, i, 0, 0)),
+            pl.BlockSpec(back[-1].shape, lambda i: (0, 0, 0)),
+            whole,
+        ],
+        out_specs=whole,
+        compiler_params=pltpu.CompilerParams(vmem_limit_bytes=58 * 1024 * 1024),
+        cost_estimate=pl.CostEstimate(flops=6 * 10**9, bytes_accessed=16 * 2**20, transcendentals=0),
+    )(last, back[-1], half)
+
+
+def fits_levels(devices):
+    return devices == 32
+
+
 def solution(mesh):
     placed = (P("set", None, "kb", None), P(), P("set", None))
+    devices = mesh.shape["kb"]
     return jax.shard_map(
-        functools.partial(local, mesh.shape["kb"]),
+        functools.partial(level_local if fits_levels(devices) else local, devices),
         mesh=mesh,
         in_specs=placed,
         out_specs=P("set", None, "kb", None),

time: 154 us -> 128 us (0.83)
  Pallas kernels: 153 us -> 128 us
    pallas_call x2, Pallas kernels: 153 us -> 128 us  [the longest x1 122 us: level_local(): pl.pallas_call(level_kernel, out_shape=[jax.ShapeDtypeStruct(result, f32)...]
where the time goes in v1:
time: 128 us
  Pallas kernels  128 us (100%)
    pallas_call x1, Pallas kernels, level_local(): pl.pallas_call(level_kernel, out_shape=[jax.ShapeDtypeStruct(result, f32)...  122 us
    pallas_call x1, Pallas kernels, level_local(): pl.pallas_call(level_finish, grid=(comps // block,), out_shape=jax.ShapeD...  6.52 us

profile of v1, /device:TPU:0, one launch (start us, length us, event | category | flops | bytes accessed | tf_op | source)
XLA Modules:
  0.0 128.0 jit_solution(12725056609137617852)
XLA Ops:
  0.0 121.5 %shard_map.73 = (f32[2,8,128,512]{3,2,1,0:T(8,128)}, f32[2,8,2,8,8,128]{5,4,3,2,1,0:T(8,128)}) custom-call(s32[2,8]{1,0:T(2,128)} %bitcast.1, s32[3,16]{1,0:T(4,128)} %mirror_ref.1, f32[2,4,128,512]{3,2,1,0:T(8,128)} %green_hbm.1, bf16[2,1024,512]{2,1,0:T(8,128)(2,1)} %constant.8.clone.time_hbm, bf16[4,512,512]{2,1,0:T(8,128)(2,1)} %constant.9.clone.plane_hbm, ...), custom_call_target="tpu_custom_call" | custom-call | flops 17999998976 | bytes 16777216 | tf_op jit(solution)/shard_map/pallas_call | solution.py:668
  121.5 6.5 %shard_map.74 = f32[2,8,128,512]{3,2,1,0:T(8,128)} custom-call(f32[2,8,2,8,8,128]{5,4,3,2,1,0:T(8,128)} %get-tuple-element.7.x_ref, bf16[2,256,1024]{2,1,0:T(8,128)(2,1)} %constant.11.clone.b_ref, f32[2,8,128,512]{3,2,1,0:T(8,128)} %get-tuple-element.8.half_ref), custom_call_target="tpu_custom_call" | custom-call | flops 6000000000 | bytes 16777216 | tf_op jit(solution)/shard_map/pallas_call | solution.py:703

commit v2 on v1

--- a/solution.py
+++ b/solution.py
@@ -334,7 +334,8 @@
 
 LEVELS = 4
 PIECES = 8
-LEAD = 3
+STACKS = (1, 3, 4)
+PARTS = 2
 GROUP = 2
 
 
@@ -380,13 +381,14 @@
 
 def level_kernel(pair_ref, mirror_ref, green_hbm, time_hbm, plane_hbm, back_hbm, half_hbm, last,
                  green, table, planes, back, mirrored, tau, x, zbuf, t, ts, chi, sent, got, acc,
-                 load, own, send, recv1, recvz, recvc, recv2):
+                 load, own, send, sendz, recv1, recvz, recvc, recv2):
     members = tau.shape[1]
     entries, slots, points = tau.shape[3:]
     side = t.shape[0]
     lines = side // LEVELS
     plane = side * side
-    comps = sent.shape[3]
+    comps = sent.shape[1] * sent.shape[4]
+    group = sent.shape[4]
     freqs = green.shape[-1]
     kept = got.shape[0]
     me = lax.axis_index("kb")
@@ -444,32 +446,37 @@
         pltpu.make_async_copy(src.at[d], dst.at[d], own_sem).wait()
         drain(dst.at[pl.ds(0, members - 1)], recv_sem)
 
-    loads[3].wait()
-    loads[0].wait()
-    stacks = table.shape[0]
-    per = PIECES // stacks
-    times = freqs // stacks
+    def finish_parts(p, dst):
+        pltpu.make_async_copy(sent.at[p, :, d], dst.at[:, d], own.at[PIECES + p]).wait()
+        drain(dst.at[:, pl.ds(0, members - 1)], recv2.at[p])
+
     dims = ((1,), (1,))
-    re = split(green[0].reshape(entries * points, freqs))
-    im = split(green[1].reshape(entries * points, freqs))
-    for s in range(stacks):
+
+    def times_of(first, count):
+        times = count * members * slots
+        base = 4 * members * slots * first
+        stack = table[base:base + 4 * times]
         outs = []
         for value in (re, im):
-            a = mm(table[s], value[0], dims)
-            outs.append(a[:2 * times] + a[2 * times:] + mm(table[s, :2 * times], value[1], dims))
+            a = mm(stack, value[0], dims)
+            outs.append(a[:2 * times] + a[2 * times:] + mm(stack[:2 * times], value[1], dims))
         both = (outs[0][:times] + outs[1][times:], outs[1][:times] - outs[0][times:])
         for part in range(2):
             for e in range(entries):
-                tau[s * per:(s + 1) * per, :, part, e] = both[part][:, e * points:(e + 1) * points].reshape(
-                    per, members, slots, points)
-        if s == 0:
-            pl.semaphore_wait(barrier, members - 1 + LEVELS - 1)
-
-        def out(p, carry):
-            exchange(tau.at[p], x.at[p], own.at[p], send.at[0], recv1.at[p])
-            return carry
-
-        lax.fori_loop(s * per, (s + 1) * per, out, 0)
+                tau[first:first + count, :, part, e] = both[part][:, e * points:(e + 1) * points].reshape(
+                    count, members, slots, points)
+
+    def exchange_times(p):
+        exchange(tau.at[p], x.at[p], own.at[p], send.at[0], recv1.at[p])
+
+    loads[3].wait()
+    re = split(green[0].reshape(entries * points, freqs))
+    im = split(green[1].reshape(entries * points, freqs))
+    loads[0].wait()
+    times_of(0, STACKS[0])
+    pl.semaphore_wait(barrier, members - 1 + LEVELS - 1)
+    exchange_times(0)
+    times_of(STACKS[0], STACKS[1])
     loads[1].wait()
     lane = lax.broadcasted_iota(jnp.int32, (plane, plane), 1)
     ry, rz = lane // side, lane % side
@@ -489,6 +496,11 @@
 
     def forward(p):
         finish(tau.at[p], x.at[p], own.at[p], recv1.at[p])
+
+        @pl.when(p + 1 < PIECES)
+        def _():
+            exchange_times(p + 1)
+
         v = x[p].reshape(lines, 2, 2, entries, slots, points)
         rows = jnp.concatenate([v[:, h, part].reshape(lines * entries * slots, points)
                                 for part in range(2) for h in range(2)], axis=1)
@@ -497,13 +509,14 @@
             for part in range(2):
                 lanes = slice(part * plane + h * points, part * plane + (h + 1) * points)
                 zbuf[p, h, z, part] = out[:, lanes].reshape(lines, entries, slots, points)
-            for level in (1, 2):
-                @pl.when(z != level)
-                def _():
-                    remote(zbuf.at[p, h, z], zbuf.at[p, h, z], send.at[1], recvz.at[p, h], level * members + d)
+
+    def send_lines(p, h):
+        for level in (1, 2):
+            @pl.when(z != level)
+            def _():
+                remote(zbuf.at[p, h, z], zbuf.at[p, h, z], sendz.at[p, h], recvz.at[p, h], level * members + d)
 
     def middle_work(p, h):
-        drain(zbuf.at[p, h, pl.ds(0, LEVELS - 1)], recvz.at[p, h])
         sigma = jnp.where(z == 1, 1.0, -1.0).astype(jnp.float32)
 
         def forth(e, carry):
@@ -531,95 +544,119 @@
             for i, pair in enumerate(dft16_half(columns, sigma)):
                 for part in range(2):
                     chi[i // lines, p, h, c, part, i % lines] = pair[part]
-            remote(chi.at[1 - mine, p, h, c], chi.at[1 - mine, p, h, c], send.at[2], recvc.at[p],
+            remote(chi.at[1 - mine, p, h, c], chi.at[1 - mine, p, h, c], send.at[1], recvc.at[p, c // group],
                    jnp.where(z == 1, 0, 3) * members + d)
             return carry
 
         lax.fori_loop(0, comps, one, 0)
 
-    def backward(p):
-        v = chi[mine, p]
-        rows = jnp.concatenate([v[h, :, part].reshape(comps * lines * slots, points)
+    def backward(p, n):
+        chosen = pl.ds(n * group, group)
+
+        @pl.when(edge)
+        def _():
+            drain(chi.at[mine, p, :, chosen], recvc.at[p, n])
+
+        v = chi[mine, p, :, n * group:(n + 1) * group]
+        rows = jnp.concatenate([v[h, :, part].reshape(group * lines * slots, points)
                                 for part in range(2) for h in range(2)], axis=1)
-        out = both_ways(rows, 2).reshape(comps, lines, slots, 2 * plane)
+        out = both_ways(rows, 2).reshape(group, lines, slots, 2 * plane)
         for q in range(lines):
             for h in range(2):
                 for part in range(2):
                     lanes = slice(part * plane + h * points, part * plane + (h + 1) * points)
-                    sent[p, 2 * q + h, part] = out[:, q, :, lanes]
+                    sent[p, n, 2 * q + h, part] = out[:, q, :, lanes]
+
+        @pl.when(p < kept)
+        def _():
+            exchange(sent.at[p, n], got.at[p, n], own.at[PIECES + p], send.at[2], recv2.at[p])
+
+        @pl.when(p >= kept)
+        def _():
+            exchange(sent.at[p, n], last.at[p - kept, n], own.at[PIECES + p], send.at[2], recv2.at[p])
+
+    def backward_all(p):
+        for n in range(PARTS):
+            backward(p, n)
 
     def frequency(m):
-        block = comps // 2
-        for i in range(2):
-            chosen = slice(i * block, (i + 1) * block)
-            value = mm3s(frequency_rows([got.at[m * GROUP + g] for g in range(GROUP)], i * block, block),
+        for i in range(PARTS):
+            chosen = slice(i * group, (i + 1) * group)
+            value = mm3s(frequency_rows([got.at[m * GROUP + g, i] for g in range(GROUP)], 0, group),
                          back[m, 0], back[m, 1])
             for part in range(2):
-                acc[part, chosen] += value[:, part * freqs:(part + 1) * freqs].reshape(block, points, freqs)
-
+                acc[part, chosen] += value[:, part * freqs:(part + 1) * freqs].reshape(group, points, freqs)
+
+    forward(0)
+    for h in range(2):
+        send_lines(0, h)
+    times_of(STACKS[0] + STACKS[1], STACKS[2])
     acc[...] = jnp.zeros(acc.shape, jnp.float32)
     loads[2].wait()
-
-    def lead(p, carry):
-        forward(p)
-        return carry
-
-    lax.fori_loop(0, LEAD, lead, 0)
+    forward(1)
 
     def step(p, carry):
-        @pl.when(p + LEAD < PIECES)
+        for h in range(2):
+            @pl.when(middle)
+            def _():
+                drain(zbuf.at[p, h, pl.ds(0, LEVELS - 1)], recvz.at[p, h])
+
+            @pl.when(edge)
+            def _():
+                drain(zbuf.at[p, h, pl.ds(0, 2)], sendz.at[p, h])
+
+            @pl.when(p + 1 < PIECES)
+            def _():
+                send_lines(p + 1, h)
+
+            @pl.when(middle)
+            def _():
+                middle_work(p, h)
+
+        @pl.when(p + 2 < PIECES)
         def _():
-            forward(p + LEAD)
+            forward(p + 2)
+
+        @pl.when(jnp.logical_or(middle, p > 0))
+        def _():
+            backward_all(jnp.where(middle, p, p - 1))
 
         @pl.when(jnp.logical_and(lax.rem(p, GROUP) == GROUP - 1, p >= 2 * GROUP - 1))
         def _():
             m = p // GROUP - 1
 
             def arrived(q, carry):
-                finish(sent.at[q], got.at[q], own.at[PIECES + q], recv2.at[q])
+                finish_parts(q, got.at[q])
                 return carry
 
             lax.fori_loop(m * GROUP, (m + 1) * GROUP, arrived, 0)
             frequency(m)
-
-        @pl.when(middle)
-        def _():
-            for h in range(2):
-                middle_work(p, h)
-
-        @pl.when(edge)
-        def _():
-            drain(chi.at[mine, p], recvc.at[p])
-
-        backward(p)
-
-        @pl.when(p < kept)
-        def _():
-            exchange(sent.at[p], got.at[p], own.at[PIECES + p], send.at[3], recv2.at[p])
-
-        @pl.when(p >= kept)
-        def _():
-            exchange(sent.at[p], last.at[p - kept], own.at[PIECES + p], send.at[3], recv2.at[p])
 
         return carry
 
     lax.fori_loop(0, PIECES, step, 0)
     store = pltpu.make_async_copy(acc, half_hbm, load.at[4])
     store.start()
-    drain(tau.at[:, pl.ds(0, members - 1)], send.at[0])
-    drain(zbuf.at[pl.ds(0, PIECES // LEVELS)], send.at[1])
 
     @pl.when(edge)
     def _():
-        drain(zbuf.at[pl.ds(0, PIECES // LEVELS)], send.at[1])
+        backward_all(PIECES - 1)
+
+    drain(tau.at[:, pl.ds(0, members - 1)], send.at[0])
 
     @pl.when(middle)
     def _():
-        drain(chi.at[0], send.at[2])
+        def gone(p, carry):
+            for h in range(2):
+                drain(zbuf.at[p, h, 0], sendz.at[p, h])
+            return carry
+
+        lax.fori_loop(0, PIECES, gone, 0)
+        drain(chi.at[0], send.at[1])
 
     for p in range(kept, PIECES):
-        finish(sent.at[p], last.at[p - kept], own.at[PIECES + p], recv2.at[p])
-    drain(sent.at[:, pl.ds(0, members - 1)], send.at[3])
+        finish_parts(p, last.at[p - kept])
+    drain(sent.at[:, :, pl.ds(0, members - 1)], send.at[2])
     store.wait()
 
 
@@ -637,7 +674,7 @@
 
 def level_finish(x_ref, b_ref, half_ref, o_ref):
     block, points, freqs = o_ref.shape[1:]
-    value = mm3s(frequency_rows([x_ref.at[g] for g in range(GROUP)], 0, block), b_ref[0], b_ref[1])
+    value = mm3s(frequency_rows([x_ref.at[g, 0] for g in range(GROUP)], 0, block), b_ref[0], b_ref[1])
     for part in range(2):
         o_ref[part] = half_ref[part] + value[:, part * freqs:(part + 1) * freqs].reshape(block, points, freqs)
 
@@ -652,17 +689,16 @@
     lines = side // LEVELS
     f32, bf16 = jnp.float32, jnp.bfloat16
     times = [piece_times(members, freqs, p) for p in range(PIECES)]
-    stacks = 2
-    per = PIECES // stacks
-    time_table = np.stack([stacked_time_table(np.concatenate(times[s * per:(s + 1) * per]), freqs)
-                           for s in range(stacks)])
+    edges = np.cumsum((0,) + STACKS)
+    time_table = np.concatenate([stacked_time_table(np.concatenate(times[a:b]), freqs)
+                                 for a, b in zip(edges[:-1], edges[1:])])
     plane_tables = np.stack(plane_table(side, 1.0) + plane_table(side, -1.0))
     groups = PIECES // GROUP
     back = [group_table(members, freqs, g) for g in range(groups)]
     early = np.stack(back[:-1])
     kept = PIECES - GROUP
     hbm = pl.BlockSpec(memory_space=pl.ANY)
-    exchanged = (members, 2, comps, slots, points)
+    exchanged = (PARTS, members, 2, comps // PARTS, slots, points)
     result = (2, comps, points, freqs)
     cells = (side, entries, 2, slots, points)
     half, last = pl.pallas_call(
@@ -687,10 +723,11 @@
             pltpu.VMEM(result, f32),
             pltpu.SemaphoreType.DMA((5,)),
             pltpu.SemaphoreType.DMA((2 * PIECES,)),
-            pltpu.SemaphoreType.DMA((4,)),
+            pltpu.SemaphoreType.DMA((3,)),
+            pltpu.SemaphoreType.DMA((PIECES, 2)),
             pltpu.SemaphoreType.DMA((PIECES,)),
             pltpu.SemaphoreType.DMA((PIECES, 2)),
-            pltpu.SemaphoreType.DMA((PIECES,)),
+            pltpu.SemaphoreType.DMA((PIECES, PARTS)),
             pltpu.SemaphoreType.DMA((PIECES,)),
         ],
         compiler_params=pltpu.CompilerParams(
@@ -705,7 +742,7 @@
         grid=(comps // block,),
         out_shape=jax.ShapeDtypeStruct(result, f32),
         in_specs=[
-            pl.BlockSpec((GROUP, members, 2, block, slots, points), lambda i: (0, 0, 0, i, 0, 0)),
+            pl.BlockSpec((GROUP, 1, members, 2, block, slots, points), lambda i: (0, i // 2, 0, 0, i % 2, 0, 0)),
             pl.BlockSpec(back[-1].shape, lambda i: (0, 0, 0)),
             whole,
         ],

time: 128 us -> 124 us (0.969)
  Pallas kernels: 128 us -> 124 us
    pallas_call x1, Pallas kernels: 122 us -> 118 us  [level_local(): pl.pallas_call(level_kernel, out_shape=[jax.ShapeDtypeStruct(result, f32)...]
where the time goes in v2:
time: 124 us
  Pallas kernels  124 us (100%)
    pallas_call x1, Pallas kernels, level_local(): pl.pallas_call(level_kernel, out_shape=[jax.ShapeDtypeStruct(result, f32)...  118 us
    pallas_call x1, Pallas kernels, level_local(): pl.pallas_call(level_finish, grid=(comps // block,), out_shape=jax.ShapeD...  6.52 us

profile of v2, /device:TPU:0, one launch (start us, length us, event | category | flops | bytes accessed | tf_op | source)
XLA Modules:
  0.0 124.1 jit_solution(879605622200739522)
XLA Ops:
  0.0 117.6 %shard_map.73 = (f32[2,8,128,512]{3,2,1,0:T(8,128)}, f32[2,2,8,2,4,8,128]{6,5,4,3,2,1,0:T(8,128)}) custom-call(s32[2,8]{1,0:T(2,128)} %bitcast.1, s32[3,16]{1,0:T(4,128)} %mirror_ref.1, f32[2,4,128,512]{3,2,1,0:T(8,128)} %green_hbm.1, bf16[2048,512]{1,0:T(8,128)(2,1)} %constant.8.clone.time_hbm, bf16[4,512,512]{2,1,0:T(8,128)(2,1)} %constant.9.clone.plane_hbm, ...), custom_call_target="tpu_custom_call" | custom-call | flops 17999998976 | bytes 16777216 | tf_op jit(solution)/shard_map/pallas_call | solution.py:704
  117.6 6.5 %shard_map.74 = f32[2,8,128,512]{3,2,1,0:T(8,128)} custom-call(f32[2,2,8,2,4,8,128]{6,5,4,3,2,1,0:T(8,128)} %get-tuple-element.7.x_ref, bf16[2,256,1024]{2,1,0:T(8,128)(2,1)} %constant.11.clone.b_ref, f32[2,8,128,512]{3,2,1,0:T(8,128)} %get-tuple-element.8.half_ref), custom_call_target="tpu_custom_call" | custom-call | flops 6000000000 | bytes 16777216 | tf_op jit(solution)/shard_map/pallas_call | solution.py:740

commit v3 on v2

--- a/solution.py
+++ b/solution.py
@@ -335,7 +335,8 @@
 LEVELS = 4
 PIECES = 8
 STACKS = (1, 3, 4)
-PARTS = 2
+PARTS = 4
+HALVES = 2
 GROUP = 2
 
 
@@ -350,9 +351,9 @@
     return np.concatenate([cos_high, sin_high, cos_low, sin_low])
 
 
-def group_table(members, freqs, group):
+def group_table(members, freqs, pieces):
     rows = []
-    for piece in range(group * GROUP, (group + 1) * GROUP):
+    for piece in pieces:
         times = piece_times(members, freqs, piece)
         angle = ((np.arange(freqs)[None, :] - freqs // 2) * (2 * times[:, None] + 1)) % (2 * freqs)
         angle = angle * (2 * np.pi / (2 * freqs))
@@ -382,8 +383,9 @@
 def level_kernel(pair_ref, mirror_ref, green_hbm, time_hbm, plane_hbm, back_hbm, half_hbm, last,
                  green, table, planes, back, mirrored, tau, x, zbuf, t, ts, chi, sent, got, acc,
                  load, own, send, sendz, recv1, recvz, recvc, recv2):
-    members = tau.shape[1]
-    entries, slots, points = tau.shape[3:]
+    members = tau.shape[2]
+    entries = green.shape[1]
+    few, slots, points = tau.shape[4:]
     side = t.shape[0]
     lines = side // LEVELS
     plane = side * side
@@ -398,10 +400,13 @@
     mine = lax.rem(z, 2)
     half = slots // 2
 
-    loads = [pltpu.make_async_copy(src, dst, load.at[i])
-             for i, (src, dst) in enumerate([(time_hbm, table), (plane_hbm, planes), (back_hbm, back),
-                                             (green_hbm, green)])]
-    for i in (3, 0, 1, 2):
+    start = 4 * members * slots * STACKS[0]
+    pairs = [(green_hbm.at[:, pl.ds(i * few, few)], green.at[:, pl.ds(i * few, few)]) for i in range(HALVES)]
+    pairs += [(time_hbm.at[pl.ds(0, start)], table.at[pl.ds(0, start)]),
+              (time_hbm.at[pl.ds(start, table.shape[0] - start)], table.at[pl.ds(start, table.shape[0] - start)]),
+              (plane_hbm, planes), (back_hbm, back)]
+    loads = [pltpu.make_async_copy(src, dst, load.at[i]) for i, (src, dst) in enumerate(pairs)]
+    for i in (0, 2, 1):
         loads[i].start()
     barrier = pltpu.get_barrier_semaphore()
 
@@ -447,37 +452,45 @@
         drain(dst.at[pl.ds(0, members - 1)], recv_sem)
 
     def finish_parts(p, dst):
-        pltpu.make_async_copy(sent.at[p, :, d], dst.at[:, d], own.at[PIECES + p]).wait()
+        pltpu.make_async_copy(sent.at[p, :, d], dst.at[:, d], own.at[PIECES + p, 0]).wait()
         drain(dst.at[:, pl.ds(0, members - 1)], recv2.at[p])
 
     dims = ((1,), (1,))
 
-    def times_of(first, count):
+    def split_entries(i):
+        return [split(green[part, i * few:(i + 1) * few].reshape(few * points, freqs)) for part in range(2)]
+
+    def times_of(first, count, i, values):
         times = count * members * slots
         base = 4 * members * slots * first
         stack = table[base:base + 4 * times]
         outs = []
-        for value in (re, im):
+        for value in values:
             a = mm(stack, value[0], dims)
             outs.append(a[:2 * times] + a[2 * times:] + mm(stack[:2 * times], value[1], dims))
         both = (outs[0][:times] + outs[1][times:], outs[1][:times] - outs[0][times:])
         for part in range(2):
-            for e in range(entries):
-                tau[first:first + count, :, part, e] = both[part][:, e * points:(e + 1) * points].reshape(
+            for e in range(few):
+                tau[first:first + count, i, :, part, e] = both[part][:, e * points:(e + 1) * points].reshape(
                     count, members, slots, points)
 
-    def exchange_times(p):
-        exchange(tau.at[p], x.at[p], own.at[p], send.at[0], recv1.at[p])
-
-    loads[3].wait()
-    re = split(green[0].reshape(entries * points, freqs))
-    im = split(green[1].reshape(entries * points, freqs))
+    def exchange_times(p, i):
+        exchange(tau.at[p, i], x.at[p, i], own.at[p, i], send.at[0], recv1.at[p, i])
+
     loads[0].wait()
-    times_of(0, STACKS[0])
-    pl.semaphore_wait(barrier, members - 1 + LEVELS - 1)
-    exchange_times(0)
-    times_of(STACKS[0], STACKS[1])
-    loads[1].wait()
+    loads[2].wait()
+    values = []
+    for i in range(HALVES):
+        if i == 1:
+            loads[1].wait()
+        values.append(split_entries(i))
+        times_of(0, STACKS[0], i, values[i])
+        if i == 0:
+            pl.semaphore_wait(barrier, members - 1 + LEVELS - 1)
+            for n in range(3, len(loads)):
+                loads[n].start()
+        exchange_times(0, i)
+    loads[4].wait()
     lane = lax.broadcasted_iota(jnp.int32, (plane, plane), 1)
     ry, rz = lane // side, lane % side
     target = (mirror_ref[1, 0] + side - ry) % side * side + (mirror_ref[2, 0] + side - rz) % side
@@ -494,33 +507,38 @@
         slot = lax.broadcasted_iota(jnp.int32, straight.shape, 0) % slots
         return jnp.where(slot < half, straight, turned)
 
-    def forward(p):
-        finish(tau.at[p], x.at[p], own.at[p], recv1.at[p])
-
-        @pl.when(p + 1 < PIECES)
-        def _():
-            exchange_times(p + 1)
-
-        v = x[p].reshape(lines, 2, 2, entries, slots, points)
-        rows = jnp.concatenate([v[:, h, part].reshape(lines * entries * slots, points)
+    def forward(p, first, count, follow=True):
+        for i in range(first, first + count):
+            finish(tau.at[p, i], x.at[p, i], own.at[p, i], recv1.at[p, i])
+
+            if follow:
+                @pl.when(p + 1 < PIECES)
+                def _():
+                    exchange_times(p + 1, i)
+
+        v = x[p, first:first + count].reshape(count, lines, 2, 2, few, slots, points)
+        rows = jnp.concatenate([v[:, :, h, part].reshape(count * lines * few * slots, points)
                                 for part in range(2) for h in range(2)], axis=1)
         out = both_ways(rows, 0)
         for h in range(2):
             for part in range(2):
                 lanes = slice(part * plane + h * points, part * plane + (h + 1) * points)
-                zbuf[p, h, z, part] = out[:, lanes].reshape(lines, entries, slots, points)
-
-    def send_lines(p, h):
-        for level in (1, 2):
-            @pl.when(z != level)
-            def _():
-                remote(zbuf.at[p, h, z], zbuf.at[p, h, z], sendz.at[p, h], recvz.at[p, h], level * members + d)
+                zbuf[p, h, first:first + count, z, part] = out[:, lanes].reshape(count, lines, few, slots, points)
+
+    def send_lines(p, h, first, count):
+        for i in range(first, first + count):
+            for level in (1, 2):
+                @pl.when(z != level)
+                def _():
+                    remote(zbuf.at[p, h, i, z], zbuf.at[p, h, i, z], sendz.at[p, h], recvz.at[p, h],
+                           level * members + d)
 
     def middle_work(p, h):
         sigma = jnp.where(z == 1, 1.0, -1.0).astype(jnp.float32)
 
         def forth(e, carry):
-            cells = [(zbuf[p, h, k // lines, 0, k % lines, e], zbuf[p, h, k // lines, 1, k % lines, e])
+            i, f = e // few, lax.rem(e, few)
+            cells = [(zbuf[p, h, i, k // lines, 0, k % lines, f], zbuf[p, h, i, k // lines, 1, k % lines, f])
                      for k in range(side)]
             for r, pair in enumerate(dft16(cells, 1)):
                 for part in range(2):
@@ -550,76 +568,83 @@
 
         lax.fori_loop(0, comps, one, 0)
 
-    def backward(p, n):
-        chosen = pl.ds(n * group, group)
-
+    def backward(p, first, count):
         @pl.when(edge)
         def _():
-            drain(chi.at[mine, p, :, chosen], recvc.at[p, n])
-
-        v = chi[mine, p, :, n * group:(n + 1) * group]
-        rows = jnp.concatenate([v[h, :, part].reshape(group * lines * slots, points)
+            for n in range(first, first + count):
+                drain(chi.at[mine, p, :, pl.ds(n * group, group)], recvc.at[p, n])
+
+        v = chi[mine, p, :, first * group:(first + count) * group]
+        rows = jnp.concatenate([v[h, :, part].reshape(count * group * lines * slots, points)
                                 for part in range(2) for h in range(2)], axis=1)
-        out = both_ways(rows, 2).reshape(group, lines, slots, 2 * plane)
+        out = both_ways(rows, 2).reshape(count, group, lines, slots, 2 * plane)
         for q in range(lines):
             for h in range(2):
                 for part in range(2):
                     lanes = slice(part * plane + h * points, part * plane + (h + 1) * points)
-                    sent[p, n, 2 * q + h, part] = out[:, q, :, lanes]
-
-        @pl.when(p < kept)
-        def _():
-            exchange(sent.at[p, n], got.at[p, n], own.at[PIECES + p], send.at[2], recv2.at[p])
-
-        @pl.when(p >= kept)
-        def _():
-            exchange(sent.at[p, n], last.at[p - kept, n], own.at[PIECES + p], send.at[2], recv2.at[p])
-
-    def backward_all(p):
-        for n in range(PARTS):
-            backward(p, n)
-
-    def frequency(m):
-        for i in range(PARTS):
-            chosen = slice(i * group, (i + 1) * group)
-            value = mm3s(frequency_rows([got.at[m * GROUP + g, i] for g in range(GROUP)], 0, group),
-                         back[m, 0], back[m, 1])
+                    sent[p, first:first + count, 2 * q + h, part] = out[:, :, q, :, lanes]
+
+        for n in range(first, first + count):
+            @pl.when(p < kept)
+            def _():
+                exchange(sent.at[p, n], got.at[p, n], own.at[PIECES + p, 0], send.at[2], recv2.at[p])
+
+            @pl.when(p >= kept)
+            def _():
+                exchange(sent.at[p, n], last.at[p - kept, n], own.at[PIECES + p, 0], send.at[2], recv2.at[p])
+
+    span = 2 * GROUP * members * slots
+
+    def frequency(pieces, first, depth):
+        block = 2 * group
+        high, low = back[0, pl.ds(first, depth)], back[1, pl.ds(first, depth)]
+        for i in range(comps // block):
+            chosen = slice(i * block, (i + 1) * block)
+            rows = frequency_rows([[got.at[p, c // group, :, :, c % group] for p in pieces]
+                                   for c in range(i * block, (i + 1) * block)])
+            value = mm3s(rows, high, low)
             for part in range(2):
-                acc[part, chosen] += value[:, part * freqs:(part + 1) * freqs].reshape(group, points, freqs)
-
-    forward(0)
-    for h in range(2):
-        send_lines(0, h)
-    times_of(STACKS[0] + STACKS[1], STACKS[2])
+                acc[part, chosen] += value[:, part * freqs:(part + 1) * freqs].reshape(block, points, freqs)
+
+    for i in range(HALVES):
+        forward(0, i, 1, False)
+        send_lines(0, 0, i, 1)
+    send_lines(0, 1, 0, HALVES)
+    loads[3].wait()
+    for i in range(HALVES):
+        times_of(STACKS[0], STACKS[1], i, values[i])
+        exchange_times(1, i)
+    for i in range(HALVES):
+        times_of(STACKS[0] + STACKS[1], STACKS[2], i, values[i])
     acc[...] = jnp.zeros(acc.shape, jnp.float32)
-    loads[2].wait()
-    forward(1)
+    forward(1, 0, HALVES)
+    loads[5].wait()
 
     def step(p, carry):
         for h in range(2):
             @pl.when(middle)
             def _():
-                drain(zbuf.at[p, h, pl.ds(0, LEVELS - 1)], recvz.at[p, h])
+                drain(zbuf.at[p, h, :, pl.ds(0, LEVELS - 1)], recvz.at[p, h])
 
             @pl.when(edge)
             def _():
-                drain(zbuf.at[p, h, pl.ds(0, 2)], sendz.at[p, h])
+                drain(zbuf.at[p, h, :, pl.ds(0, 2)], sendz.at[p, h])
 
             @pl.when(p + 1 < PIECES)
             def _():
-                send_lines(p + 1, h)
+                send_lines(p + 1, h, 0, HALVES)
 
             @pl.when(middle)
             def _():
                 middle_work(p, h)
 
+            @pl.when(middle if h == 1 else jnp.logical_and(edge, p > 0))
+            def _():
+                backward(p if h == 1 else p - 1, 0, PARTS)
+
         @pl.when(p + 2 < PIECES)
         def _():
-            forward(p + 2)
-
-        @pl.when(jnp.logical_or(middle, p > 0))
-        def _():
-            backward_all(jnp.where(middle, p, p - 1))
+            forward(p + 2, 0, HALVES)
 
         @pl.when(jnp.logical_and(lax.rem(p, GROUP) == GROUP - 1, p >= 2 * GROUP - 1))
         def _():
@@ -630,53 +655,79 @@
                 return carry
 
             lax.fori_loop(m * GROUP, (m + 1) * GROUP, arrived, 0)
-            frequency(m)
+            frequency([m * GROUP + g for g in range(GROUP)], m * span, span)
 
         return carry
 
     lax.fori_loop(0, PIECES, step, 0)
-    store = pltpu.make_async_copy(acc, half_hbm, load.at[4])
-    store.start()
+    end = PIECES - 1
 
     @pl.when(edge)
     def _():
-        backward_all(PIECES - 1)
-
-    drain(tau.at[:, pl.ds(0, members - 1)], send.at[0])
+        backward(end, 0, 2)
+
+    finish_parts(end - 1, got.at[end - 1])
+    frequency([end - 1], back.shape[1] - span // GROUP, span // GROUP)
+    store = pltpu.make_async_copy(acc, half_hbm, load.at[7])
+    store.start()
+
+    @pl.when(edge)
+    def _():
+        for n in range(2, PARTS):
+            backward(end, n, 1)
+
+    drain(tau.at[:, :, pl.ds(0, members - 1)], send.at[0])
 
     @pl.when(middle)
     def _():
         def gone(p, carry):
             for h in range(2):
-                drain(zbuf.at[p, h, 0], sendz.at[p, h])
+                drain(zbuf.at[p, h, :, 0], sendz.at[p, h])
             return carry
 
         lax.fori_loop(0, PIECES, gone, 0)
         drain(chi.at[0], send.at[1])
 
-    for p in range(kept, PIECES):
-        finish_parts(p, last.at[p - kept])
+    finish_parts(end, last.at[end - kept])
     drain(sent.at[:, :, pl.ds(0, members - 1)], send.at[2])
     store.wait()
 
 
-def frequency_rows(pieces, first, block):
+def frequency_rows(blocks):
     rows = []
-    for c in range(first, first + block):
+    for pieces in blocks:
         parts = []
         for ref in pieces:
             for part in range(2):
-                v = ref[:, part, c]
+                v = ref[:, part]
                 parts.append(v.reshape(v.shape[0] * v.shape[1], v.shape[2]))
         rows.append(jnp.concatenate(parts, axis=0).T)
     return jnp.concatenate(rows, axis=0)
 
 
-def level_finish(x_ref, b_ref, half_ref, o_ref):
-    block, points, freqs = o_ref.shape[1:]
-    value = mm3s(frequency_rows([x_ref.at[g, 0] for g in range(GROUP)], 0, block), b_ref[0], b_ref[1])
-    for part in range(2):
-        o_ref[part] = half_ref[part] + value[:, part * freqs:(part + 1) * freqs].reshape(block, points, freqs)
+def level_finish(x_hbm, b_hbm, half_hbm, o_hbm, x, b_ref, total, sem):
+    points, freqs = total.shape[2:]
+    group = x.shape[3]
+    spans = [pl.ds(n * group, group) for n in range(PARTS)]
+    ahead = [pltpu.make_async_copy(x_hbm.at[0, n], x.at[n], sem.at[0, n]) for n in range(PARTS)]
+    halves = [pltpu.make_async_copy(half_hbm.at[:, span], total.at[:, span], sem.at[1, n])
+              for n, span in enumerate(spans)]
+    stores = [pltpu.make_async_copy(total.at[:, span], o_hbm.at[:, span], sem.at[2, n])
+              for n, span in enumerate(spans)]
+    tables = pltpu.make_async_copy(b_hbm, b_ref, sem.at[3, 0])
+    for copy in [tables] + ahead + halves:
+        copy.start()
+    tables.wait()
+    for n in range(PARTS):
+        chosen = slice(n * group, (n + 1) * group)
+        ahead[n].wait()
+        value = mm3s(frequency_rows([[x.at[n, :, :, c]] for c in range(group)]), b_ref[0], b_ref[1])
+        halves[n].wait()
+        for part in range(2):
+            total[part, chosen] += value[:, part * freqs:(part + 1) * freqs].reshape(group, points, freqs)
+        stores[n].start()
+    for store in stores:
+        store.wait()
 
 
 def level_local(devices, green, pair_table, mirror_map):
@@ -687,6 +738,7 @@
     members = devices // LEVELS
     slots = freqs // (members * PIECES)
     lines = side // LEVELS
+    few = entries // HALVES
     f32, bf16 = jnp.float32, jnp.bfloat16
     times = [piece_times(members, freqs, p) for p in range(PIECES)]
     edges = np.cumsum((0,) + STACKS)
@@ -694,16 +746,17 @@
                                  for a, b in zip(edges[:-1], edges[1:])])
     plane_tables = np.stack(plane_table(side, 1.0) + plane_table(side, -1.0))
     groups = PIECES // GROUP
-    back = [group_table(members, freqs, g) for g in range(groups)]
-    early = np.stack(back[:-1])
-    kept = PIECES - GROUP
+    early = np.concatenate([group_table(members, freqs, range(g * GROUP, (g + 1) * GROUP)) for g in range(groups - 1)]
+                           + [group_table(members, freqs, [PIECES - 2])], axis=1)
+    final = group_table(members, freqs, [PIECES - 1])
+    kept = PIECES - 1
     hbm = pl.BlockSpec(memory_space=pl.ANY)
     exchanged = (PARTS, members, 2, comps // PARTS, slots, points)
     result = (2, comps, points, freqs)
     cells = (side, entries, 2, slots, points)
     half, last = pl.pallas_call(
         level_kernel,
-        out_shape=[jax.ShapeDtypeStruct(result, f32), jax.ShapeDtypeStruct((GROUP,) + exchanged, f32)],
+        out_shape=[jax.ShapeDtypeStruct(result, f32), jax.ShapeDtypeStruct((1,) + exchanged, f32)],
         in_specs=[SMEM, SMEM, hbm, hbm, hbm, hbm],
         out_specs=[hbm, hbm],
         scratch_shapes=[
@@ -712,20 +765,20 @@
             pltpu.VMEM(plane_tables.shape, bf16),
             pltpu.VMEM(early.shape, bf16),
             pltpu.VMEM(plane_tables.shape, bf16),
-            pltpu.VMEM((PIECES, members, 2, entries, slots, points), f32),
-            pltpu.VMEM((PIECES, members, 2, entries, slots, points), f32),
-            pltpu.VMEM((PIECES, 2, LEVELS, 2, lines, entries, slots, points), f32),
+            pltpu.VMEM((PIECES, HALVES, members, 2, few, slots, points), f32),
+            pltpu.VMEM((PIECES, HALVES, members, 2, few, slots, points), f32),
+            pltpu.VMEM((PIECES, 2, HALVES, LEVELS, 2, lines, few, slots, points), f32),
             pltpu.VMEM(cells, f32),
             pltpu.VMEM(cells, f32),
             pltpu.VMEM((2, PIECES, 2, comps, 2, lines, slots, points), f32),
             pltpu.VMEM((PIECES,) + exchanged, f32),
             pltpu.VMEM((kept,) + exchanged, f32),
             pltpu.VMEM(result, f32),
-            pltpu.SemaphoreType.DMA((5,)),
-            pltpu.SemaphoreType.DMA((2 * PIECES,)),
+            pltpu.SemaphoreType.DMA((8,)),
+            pltpu.SemaphoreType.DMA((2 * PIECES, HALVES)),
             pltpu.SemaphoreType.DMA((3,)),
             pltpu.SemaphoreType.DMA((PIECES, 2)),
-            pltpu.SemaphoreType.DMA((PIECES,)),
+            pltpu.SemaphoreType.DMA((PIECES, HALVES)),
             pltpu.SemaphoreType.DMA((PIECES, 2)),
             pltpu.SemaphoreType.DMA((PIECES, PARTS)),
             pltpu.SemaphoreType.DMA((PIECES,)),
@@ -735,21 +788,20 @@
         ),
         cost_estimate=pl.CostEstimate(flops=18 * 10**9, bytes_accessed=16 * 2**20, transcendentals=0),
     )(pair_table.T, mirror_map, green, time_table, plane_tables, early)
-    block = comps // 4
-    whole = pl.BlockSpec((2, block, points, freqs), lambda i: (0, i, 0, 0))
     return pl.pallas_call(
         level_finish,
-        grid=(comps // block,),
         out_shape=jax.ShapeDtypeStruct(result, f32),
-        in_specs=[
-            pl.BlockSpec((GROUP, 1, members, 2, block, slots, points), lambda i: (0, i // 2, 0, 0, i % 2, 0, 0)),
-            pl.BlockSpec(back[-1].shape, lambda i: (0, 0, 0)),
-            whole,
+        in_specs=[hbm, hbm, hbm],
+        out_specs=hbm,
+        scratch_shapes=[
+            pltpu.VMEM(exchanged, f32),
+            pltpu.VMEM(final.shape, bf16),
+            pltpu.VMEM(result, f32),
+            pltpu.SemaphoreType.DMA((4, PARTS)),
         ],
-        out_specs=whole,
-        compiler_params=pltpu.CompilerParams(vmem_limit_bytes=58 * 1024 * 1024),
+        compiler_params=pltpu.CompilerParams(vmem_limit_bytes=60 * 1024 * 1024),
         cost_estimate=pl.CostEstimate(flops=6 * 10**9, bytes_accessed=16 * 2**20, transcendentals=0),
-    )(last, back[-1], half)
+    )(last, final, half)
 
 
 def fits_levels(devices):

time: 124 us -> 122 us (0.984)
  Pallas kernels: 124 us -> 122 us
    pallas_call x1, Pallas kernels: 6.52 us -> 5.01 us  [level_local(): pl.pallas_call(level_finish, out_shape=jax.ShapeDtypeStruct(result, f32),...]
where the time goes in v3:
time: 122 us
  Pallas kernels  122 us (100%)
    pallas_call x1, Pallas kernels, level_local(): pl.pallas_call(level_kernel, out_shape=[jax.ShapeDtypeStruct(result, f32)...  117 us
    pallas_call x1, Pallas kernels, level_local(): pl.pallas_call(level_finish, out_shape=jax.ShapeDtypeStruct(result, f32),...  5.01 us

profile of v3, /device:TPU:0, one launch (start us, length us, event | category | flops | bytes accessed | tf_op | source)
XLA Modules:
  0.0 122.2 jit_solution(877219457028688669)
XLA Ops:
  0.0 117.2 %shard_map.73 = (f32[2,8,128,512]{3,2,1,0:T(8,128)}, f32[1,4,8,2,2,8,128]{6,5,4,3,2,1,0:T(8,128)}) custom-call(s32[2,8]{1,0:T(2,128)} %bitcast.1, s32[3,16]{1,0:T(4,128)} %mirror_ref.1, f32[2,4,128,512]{3,2,1,0:T(8,128)} %green_hbm.1, bf16[2048,512]{1,0:T(8,128)(2,1)} %constant.8.clone.time_hbm, bf16[4,512,512]{2,1,0:T(8,128)(2,1)} %constant.9.clone.plane_hbm, ...), custom_call_target="tpu_custom_call" | custom-call | flops 17999998976 | bytes 16777216 | tf_op jit(solution)/shard_map/pallas_call | solution.py:757
  117.2 5.0 %shard_map.74 = f32[2,8,128,512]{3,2,1,0:T(8,128)} custom-call(f32[1,4,8,2,2,8,128]{6,5,4,3,2,1,0:T(8,128)} %get-tuple-element.7.x_hbm, bf16[2,128,1024]{2,1,0:T(8,128)(2,1)} %constant.11.clone.b_hbm, f32[2,8,128,512]{3,2,1,0:T(8,128)} %get-tuple-element.8.half_hbm), custom_call_target="tpu_custom_call" | custom-call | flops 6000000000 | bytes 16777216 | tf_op jit(solution)/shard_map/pallas_call | solution.py:791

commit v4 on v3

--- a/solution.py
+++ b/solution.py
@@ -380,8 +380,8 @@
     return out
 
 
-def level_kernel(pair_ref, mirror_ref, green_hbm, time_hbm, plane_hbm, back_hbm, half_hbm, last,
-                 green, table, planes, back, mirrored, tau, x, zbuf, t, ts, chi, sent, got, acc,
+def level_kernel(pair_hbm, mirror_hbm, green_hbm, time_hbm, plane_hbm, back_hbm, half_hbm, last,
+                 pair_ref, mirror_ref, green, table, planes, back, mirrored, tau, x, zbuf, t, ts, chi, sent, got, acc,
                  load, own, send, sendz, recv1, recvz, recvc, recv2):
     members = tau.shape[2]
     entries = green.shape[1]
@@ -401,6 +401,8 @@
     half = slots // 2
 
     start = 4 * members * slots * STACKS[0]
+    pairs = [(pair_hbm, pair_ref), (mirror_hbm, mirror_ref)]
+    small = [pltpu.make_async_copy(src, dst, load.at[8 + i]) for i, (src, dst) in enumerate(pairs)]
     pairs = [(green_hbm.at[:, pl.ds(i * few, few)], green.at[:, pl.ds(i * few, few)]) for i in range(HALVES)]
     pairs += [(time_hbm.at[pl.ds(0, start)], table.at[pl.ds(0, start)]),
               (time_hbm.at[pl.ds(start, table.shape[0] - start)], table.at[pl.ds(start, table.shape[0] - start)]),
@@ -408,6 +410,8 @@
     loads = [pltpu.make_async_copy(src, dst, load.at[i]) for i, (src, dst) in enumerate(pairs)]
     for i in (0, 2, 1):
         loads[i].start()
+    for copy in small:
+        copy.start()
     barrier = pltpu.get_barrier_semaphore()
 
     def greet(other):
@@ -491,6 +495,8 @@
                 loads[n].start()
         exchange_times(0, i)
     loads[4].wait()
+    for copy in small:
+        copy.wait()
     lane = lax.broadcasted_iota(jnp.int32, (plane, plane), 1)
     ry, rz = lane // side, lane % side
     target = (mirror_ref[1, 0] + side - ry) % side * side + (mirror_ref[2, 0] + side - rz) % side
@@ -666,16 +672,15 @@
     def _():
         backward(end, 0, 2)
 
+    @pl.when(edge)
+    def _():
+        for n in range(2, PARTS):
+            backward(end, n, 1)
+
     finish_parts(end - 1, got.at[end - 1])
     frequency([end - 1], back.shape[1] - span // GROUP, span // GROUP)
     store = pltpu.make_async_copy(acc, half_hbm, load.at[7])
     store.start()
-
-    @pl.when(edge)
-    def _():
-        for n in range(2, PARTS):
-            backward(end, n, 1)
-
     drain(tau.at[:, :, pl.ds(0, members - 1)], send.at[0])
 
     @pl.when(middle)
@@ -757,9 +762,11 @@
     half, last = pl.pallas_call(
         level_kernel,
         out_shape=[jax.ShapeDtypeStruct(result, f32), jax.ShapeDtypeStruct((1,) + exchanged, f32)],
-        in_specs=[SMEM, SMEM, hbm, hbm, hbm, hbm],
+        in_specs=[hbm] * 6,
         out_specs=[hbm, hbm],
         scratch_shapes=[
+            pltpu.SMEM((2, comps), jnp.int32),
+            pltpu.SMEM(mirror_map.shape, jnp.int32),
             pltpu.VMEM(green.shape, f32),
             pltpu.VMEM(time_table.shape, bf16),
             pltpu.VMEM(plane_tables.shape, bf16),
@@ -774,7 +781,7 @@
             pltpu.VMEM((PIECES,) + exchanged, f32),
             pltpu.VMEM((kept,) + exchanged, f32),
             pltpu.VMEM(result, f32),
-            pltpu.SemaphoreType.DMA((8,)),
+            pltpu.SemaphoreType.DMA((10,)),
             pltpu.SemaphoreType.DMA((2 * PIECES, HALVES)),
             pltpu.SemaphoreType.DMA((3,)),
             pltpu.SemaphoreType.DMA((PIECES, 2)),

time: 122 us -> 120 us (0.984)
  Pallas kernels: 122 us -> 120 us
    pallas_call x1, Pallas kernels: 117 us -> 115 us  [level_local(): pl.pallas_call(level_kernel, out_shape=[jax.ShapeDtypeStruct(result, f32)...]
where the time goes in v4:
time: 120 us
  Pallas kernels  120 us (100%)
    pallas_call x1, Pallas kernels, level_local(): pl.pallas_call(level_kernel, out_shape=[jax.ShapeDtypeStruct(result, f32)...  115 us
    pallas_call x1, Pallas kernels, level_local(): pl.pallas_call(level_finish, out_shape=jax.ShapeDtypeStruct(result, f32),...  5.01 us

profile of v4, /device:TPU:0, one launch (start us, length us, event | category | flops | bytes accessed | tf_op | source)
XLA Modules:
  0.0 120.3 jit_solution(11680963182697473722)
XLA Ops:
  0.0 115.2 %shard_map.73 = (f32[2,8,128,512]{3,2,1,0:T(8,128)}, f32[1,4,8,2,2,8,128]{6,5,4,3,2,1,0:T(8,128)}) custom-call(s32[2,8]{1,0:T(2,128)} %bitcast.1, s32[3,16]{1,0:T(4,128)} %mirror_hbm.1, f32[2,4,128,512]{3,2,1,0:T(8,128)} %green_hbm.1, bf16[2048,512]{1,0:T(8,128)(2,1)} %constant.8.clone.time_hbm, bf16[4,512,512]{2,1,0:T(8,128)(2,1)} %constant.9.clone.plane_hbm, ...), custom_call_target="tpu_custom_call" | custom-call | flops 17999998976 | bytes 16777216 | tf_op jit(solution)/shard_map/pallas_call | solution.py:762
  115.3 5.0 %shard_map.74 = f32[2,8,128,512]{3,2,1,0:T(8,128)} custom-call(f32[1,4,8,2,2,8,128]{6,5,4,3,2,1,0:T(8,128)} %get-tuple-element.7.x_hbm, bf16[2,128,1024]{2,1,0:T(8,128)(2,1)} %constant.11.clone.b_hbm, f32[2,8,128,512]{3,2,1,0:T(8,128)} %get-tuple-element.8.half_hbm), custom_call_target="tpu_custom_call" | custom-call | flops 6000000000 | bytes 16777216 | tf_op jit(solution)/shard_map/pallas_call | solution.py:798

commit v5 on v4

--- a/solution.py
+++ b/solution.py
@@ -446,7 +446,8 @@
             remote(src.at[other], dst.at[d], send_sem, recv_sem, z * members + other)
             return carry
 
-        lax.fori_loop(1, members, one, 0)
+        for i in range(1, members):
+            one(i, 0)
 
     def drain(ref, sem):
         pltpu.make_async_copy(ref, ref, sem).wait()
@@ -615,11 +616,11 @@
     for i in range(HALVES):
         forward(0, i, 1, False)
         send_lines(0, 0, i, 1)
-    send_lines(0, 1, 0, HALVES)
     loads[3].wait()
     for i in range(HALVES):
         times_of(STACKS[0], STACKS[1], i, values[i])
         exchange_times(1, i)
+    send_lines(0, 1, 0, HALVES)
     for i in range(HALVES):
         times_of(STACKS[0] + STACKS[1], STACKS[2], i, values[i])
     acc[...] = jnp.zeros(acc.shape, jnp.float32)
@@ -670,7 +671,8 @@
 
     @pl.when(edge)
     def _():
-        backward(end, 0, 2)
+        backward(end, 0, 1)
+        backward(end, 1, 1)
 
     @pl.when(edge)
     def _():

time: 120 us -> 120 us (level)
  no operation moved by 1% of the time
where the time goes in v5:
time: 120 us
  Pallas kernels  120 us (100%)
    pallas_call x1, Pallas kernels, level_local(): pl.pallas_call(level_kernel, out_shape=[jax.ShapeDtypeStruct(result, f32)...  115 us
    pallas_call x1, Pallas kernels, level_local(): pl.pallas_call(level_finish, out_shape=jax.ShapeDtypeStruct(result, f32),...  5.01 us

profile of v5, /device:TPU:0, one launch (start us, length us, event | category | flops | bytes accessed | tf_op | source)
XLA Modules:
  0.0 119.6 jit_solution(15753209766544628379)
XLA Ops:
  0.0 114.5 %shard_map.73 = (f32[2,8,128,512]{3,2,1,0:T(8,128)}, f32[1,4,8,2,2,8,128]{6,5,4,3,2,1,0:T(8,128)}) custom-call(s32[2,8]{1,0:T(2,128)} %bitcast.1, s32[3,16]{1,0:T(4,128)} %mirror_hbm.1, f32[2,4,128,512]{3,2,1,0:T(8,128)} %green_hbm.1, bf16[2048,512]{1,0:T(8,128)(2,1)} %constant.8.clone.time_hbm, bf16[4,512,512]{2,1,0:T(8,128)(2,1)} %constant.9.clone.plane_hbm, ...), custom_call_target="tpu_custom_call" | custom-call | flops 17999998976 | bytes 16777216 | tf_op jit(solution)/shard_map/pallas_call | solution.py:764
  114.5 5.0 %shard_map.74 = f32[2,8,128,512]{3,2,1,0:T(8,128)} custom-call(f32[1,4,8,2,2,8,128]{6,5,4,3,2,1,0:T(8,128)} %get-tuple-element.7.x_hbm, bf16[2,128,1024]{2,1,0:T(8,128)(2,1)} %constant.11.clone.b_hbm, f32[2,8,128,512]{3,2,1,0:T(8,128)} %get-tuple-element.8.half_hbm), custom_call_target="tpu_custom_call" | custom-call | flops 6000000000 | bytes 16777216 | tf_op jit(solution)/shard_map/pallas_call | solution.py:800

commit v6 on v5

--- a/solution.py
+++ b/solution.py
@@ -334,7 +334,7 @@
 
 LEVELS = 4
 PIECES = 8
-STACKS = (1, 3, 4)
+STACKS = (1, 1, 6)
 PARTS = 4
 HALVES = 2
 GROUP = 2

time: 120 us -> 119 us (level)
  no operation moved by 1% of the time
where the time goes in v6:
time: 119 us
  Pallas kernels  119 us (100%)
    pallas_call x1, Pallas kernels, level_local(): pl.pallas_call(level_kernel, out_shape=[jax.ShapeDtypeStruct(result, f32)...  114 us
    pallas_call x1, Pallas kernels, level_local(): pl.pallas_call(level_finish, out_shape=jax.ShapeDtypeStruct(result, f32),...  5.01 us

profile of v6, /device:TPU:0, one launch (start us, length us, event | category | flops | bytes accessed | tf_op | source)
XLA Modules:
  0.0 118.8 jit_solution(6142752563454407746)
XLA Ops:
  0.0 113.8 %shard_map.73 = (f32[2,8,128,512]{3,2,1,0:T(8,128)}, f32[1,4,8,2,2,8,128]{6,5,4,3,2,1,0:T(8,128)}) custom-call(s32[2,8]{1,0:T(2,128)} %bitcast.1, s32[3,16]{1,0:T(4,128)} %mirror_hbm.1, f32[2,4,128,512]{3,2,1,0:T(8,128)} %green_hbm.1, bf16[2048,512]{1,0:T(8,128)(2,1)} %constant.8.clone.time_hbm, bf16[4,512,512]{2,1,0:T(8,128)(2,1)} %constant.9.clone.plane_hbm, ...), custom_call_target="tpu_custom_call" | custom-call | flops 17999998976 | bytes 16777216 | tf_op jit(solution)/shard_map/pallas_call | solution.py:764
  113.8 5.0 %shard_map.74 = f32[2,8,128,512]{3,2,1,0:T(8,128)} custom-call(f32[1,4,8,2,2,8,128]{6,5,4,3,2,1,0:T(8,128)} %get-tuple-element.7.x_hbm, bf16[2,128,1024]{2,1,0:T(8,128)(2,1)} %constant.11.clone.b_hbm, f32[2,8,128,512]{3,2,1,0:T(8,128)} %get-tuple-element.8.half_hbm), custom_call_target="tpu_custom_call" | custom-call | flops 6000000000 | bytes 16777216 | tf_op jit(solution)/shard_map/pallas_call | solution.py:800
